TPU v7x, 512 devices: a whole 4x4x16 slice. The times are simulated.
512 devices in a mesh: band: 32 (over y, z_lo, core), ga: 16 (over z_hi, x).
Axes of the slice: x: 4, y: 4, z: 16 (z_hi: 4, z_lo: 4; z = z_hi * 4 + z_lo), core: 2. Of those that a mesh axis runs over, the one named last changes fastest.
Arguments:
- coefficients: bfloat16 [2, 64, 4096, 128], P(None, 'band', 'ga'), may hold values from -6 to 6
- panel: bfloat16 [2, 64, 4096, 128], P(None, 'band', 'ga'), may hold values from -6 to 6
- potential: float32 [128, 128, 128], P('ga'), may hold values from -6 to 6
- stick_columns: int32 [4096], replicated, may hold values from 0 to 16383, as said below
Outputs:
- applied: bfloat16 [2, 64, 4096, 128], P(None, 'band', 'ga')
- intersection: float32 [2, 64, 64], P(None, 'band', 'ga')
Inputs may be any that keep to these rules, and one draw needn't show every extreme that they name: `stick_columns`: 4096 distinct grid columns, in ascending order.
All inputs are finite; a program needn't handle non-finite values.
Results may differ from a plain program's by a relative error of at most 0.014.
Values may be sent and summed in bfloat16 or wider, within the bound.
A program may use at most 128 MiB of HBM per device.

v0:
```python
import math

import jax
import jax.numpy as jnp
from jax import lax
from jax.sharding import PartitionSpec as P


def section_tables(length, orient):
    counter = jnp.arange(length, dtype=jnp.int32)
    phases = counter[:, None] * counter[None, :] % length
    angles = phases.astype(jnp.float32) * (2.0 * math.pi / length)
    cosine = jnp.cos(angles)
    sine = jnp.sin(angles) * orient
    from_real = jnp.stack([cosine, sine], axis=1)
    from_imag = jnp.stack([-sine, cosine], axis=1)
    return jnp.stack([from_real, from_imag]).astype(jnp.bfloat16)


def section(pattern, operand, table):
    return jnp.einsum(pattern, operand, table, preferred_element_type=jnp.float32)


def intersection_terms(first_op, second_op, spread):
    numbers = (((1,), (1,)), ((), ()))

    def contract(one_side, other_side):
        return lax.dot_general(one_side, other_side, numbers, preferred_element_type=jnp.float32)

    real_part = contract(first_op[0], second_op[0]) + contract(first_op[1], second_op[1])
    imag_part = contract(first_op[0], second_op[1]) - contract(first_op[1], second_op[0])
    return jnp.stack([real_part, imag_part]) * spread


def per_device(coefficients, panel, potential, stick_columns):
    depth = coefficients.shape[3]
    local_sticks = coefficients.shape[2]
    extent_x = potential.shape[1]
    extent_y = potential.shape[2]
    all_sticks = stick_columns.shape[0]
    spread = 1.0 / math.sqrt(all_sticks * depth)
    grid_scale = 1.0 / math.sqrt(extent_x * extent_y * depth)
    ztable_in = section_tables(depth, 1.0)
    ytable_in = section_tables(extent_y, 1.0)
    xtable_in = section_tables(extent_x, 1.0)
    ztable_out = section_tables(depth, -1.0)
    ytable_out = section_tables(extent_y, -1.0)
    xtable_out = section_tables(extent_x, -1.0)
    columns_z = (section("cbsk,ckez->ebzs", coefficients, ztable_in) * spread).astype(jnp.bfloat16)
    slot_index = (
        jnp.full((extent_x * extent_y,), all_sticks, jnp.int32)
        .at[stick_columns]
        .set(jnp.arange(all_sticks, dtype=jnp.int32))
    )
    present = slot_index < all_sticks
    safe_index = jnp.minimum(slot_index, all_sticks - 1)
    received = lax.all_to_all(columns_z, "ga", split_axis=2, concat_axis=3, tiled=True)
    members = received.shape[1]
    layers = received.shape[2]
    planes = jnp.where(present, jnp.take(received, safe_index, axis=3), jnp.zeros((), jnp.bfloat16))
    planes = planes.reshape(2, members, layers, extent_x, extent_y)
    level = section("cmlxy,cyek->emlxk", planes, ytable_in).astype(jnp.bfloat16)
    product = (section("cmlxy,cxek->emlky", level, xtable_in) * potential).astype(jnp.bfloat16)
    level = section("cmlxy,cyek->emlxk", product, ytable_out).astype(jnp.bfloat16)
    final = section("cmlxy,cxek->emlky", level, xtable_out) * grid_scale
    flattened = final.reshape(2, members, layers, extent_x * extent_y)
    mixed = jnp.take(flattened, stick_columns, axis=3).astype(jnp.bfloat16)
    mixed = lax.all_to_all(mixed, "ga", split_axis=3, concat_axis=2, tiled=True)
    applied = section("cbzs,czek->ebsk", mixed, ztable_out).astype(jnp.bfloat16)
    own_block = applied.reshape(2, applied.shape[1], local_sticks * depth)
    shards = lax.all_gather(panel, "band", axis=1, tiled=True)
    flat_panel = shards.reshape(2, shards.shape[1], local_sticks * depth)
    partial_value = intersection_terms(flat_panel, own_block, spread)
    partial_value = lax.all_to_all(partial_value, "band", split_axis=1, concat_axis=2, tiled=True)
    intersection = lax.psum_scatter(partial_value, "ga", scatter_dimension=2, tiled=True)
    return (applied, intersection)


def solution(mesh):
    in_specs = (P(None, "band", "ga", None), P(None, "band", "ga", None), P("ga", None, None), P())
    out_specs = (P(None, "band", "ga", None), P(None, "band", "ga"))
    return jax.shard_map(
        per_device, mesh=mesh, in_specs=in_specs, out_specs=out_specs, check_vma=False
    )
```

profile of v0, /device:TPU:1, one launch (start us, length us, event | category | flops | bytes accessed | tf_op | source)
XLA Modules:
  0.0 426.1 jit_solution(14974401145846118719)
XLA Ops:
  7.2 1.7 copy.47
  9.8 1.2 fusion.13
  11.0 1.0 copy.36
  12.0 18.2 %all-to-all-start = ((bf16[2,2,128,256]{3,1,0,2:T(2,128)(2,1)}), bf16[2,2,128,256]{3,1,0,2:T(2,128)(2,1)S(1)}, u32[]{:S(2)}, u32[]{:S(2)}) async-start(bf16[2,2,128,256]{3,1,0,2:T(2,128)(2,1)} %copy.36), calls=%async_computation | async-start | bytes 524288 | tf_op jit(solution)/shard_map/all_to_all | solution.py:57
  30.9 15.5 %scatter_custom_fusion = s32[16384]{0:T(1024)S(1)} fusion(s32[4096]{0:T(1024)S(1)} %get-tuple-element.21, s32[4096]{0:T(1024)S(1)} %iota.43, s32[]{:T(128)} %constant.68.clone.1), kind=kCustom, calls=%fused_computation.85 | custom fusion | bytes 65540 | tf_op jit(solution)/shard_map/scatter | solution.py:53
  47.3 7.3 %copy.37 = bf16[2,2,16,8,256]{3,1,4,2,0:T(2,128)(2,1)} copy(bf16[2,2,16,8,256]{4,1,0,3,2:T(2,128)(2,1)S(1)} %bitcast.209) | data formatting | bytes 524288 | tf_op jit(solution)/shard_map/all_to_all | solution.py:57
  54.6 133.9 %gather_fusion = bf16[16384,2,2,8]{3,2,1,0:T(2,128)(2,1)} fusion(bf16[2,2,8,4096]{2,1,3,0:T(2,128)(2,1)} %bitcast.208, s32[16384]{0:T(1024)S(1)} %fusion.59), kind=kCustom, calls=%fused_computation | custom fusion | bytes 2162688 | tf_op jit(solution)/shard_map/jit(_take)/gather | solution.py:60
  188.5 23.0 %copy.38 = bf16[2,2,8,128,128]{4,3,0,2,1:T(8,128)(2,1)S(1)} copy(bf16[2,2,8,128,128]{2,1,0,4,3:T(2,128)(2,1)} %bitcast.205) | data formatting | bytes 2097152 | tf_op jit(solution)/shard_map/jit(_take)/gather | solution.py:60
  213.1 17.7 %copy.83 = bf16[2,2,8,128,128]{2,1,4,3,0:T(2,128)(2,1)} copy(bf16[2,2,8,128,128]{4,3,2,1,0:T(8,128)(2,1)S(1)} %fusion.6) | data formatting | bytes 2097152 | tf_op jit(solution)/shard_map/reshape | solution.py:66
  230.8 39.1 %gather_fusion.1 = bf16[4096,2,2,8]{3,2,1,0:T(2,128)(2,1)} fusion(bf16[2,2,8,16384]{2,1,3,0:T(2,128)(2,1)} %bitcast.206, s32[4096]{0:T(1024)S(1)} %get-tuple-element.20), kind=kCustom, calls=%fused_computation.1 | custom fusion | bytes 540672 | tf_op jit(solution)/shard_map/jit(_take)/gather | solution.py:67
  269.9 16.7 %fusion.72 = bf16[4096,2,2,8]{3,2,1,0:T(2,128)(2,1)} fusion(bf16[4096,2,2,8]{3,2,1,0:T(2,128)(2,1)} %gather_fusion.1, pred[4096]{0:T(1024)(128)(4,1)S(1)} %compare_and_fusion), kind=kLoop, calls=%fused_computation.98 | loop fusion | flops 131072 | bytes 528384
  286.6 5.8 %reshape.200 = bf16[16,2,4096]{2,1,0:T(2,128)(2,1)S(1)} reshape(bf16[4096,2,2,8]{3,2,1,0:T(2,128)(2,1)} %fusion.72) | data formatting | bytes 524288
  292.4 28.8 %all_to_all.54 = bf16[16,2,4096]{2,1,0:T(2,128)(2,1)S(1)} all-to-all(bf16[16,2,4096]{2,1,0:T(2,128)(2,1)S(1)} %reshape.200), channel_id=1, replica_groups=mesh['band'=32,'ga'=16] {'ga'}, dimensions={0} | all-to-all | bytes 524288 | tf_op jit(solution)/shard_map/all_to_all | solution.py:68
  321.1 5.9 %reshape.201 = bf16[4096,2,2,8]{3,2,1,0:T(2,128)(2,1)} reshape(bf16[16,2,4096]{2,1,0:T(2,128)(2,1)S(1)} %all_to_all.54) | data formatting | bytes 524288
  327.1 8.9 %copy.45 = bf16[2,2,8,16,256]{4,2,3,0,1:T(8,128)(2,1)S(1)} copy(bf16[2,2,8,16,256]{2,1,0,4,3:T(2,128)(2,1)} %bitcast.207) | data formatting | bytes 524288 | tf_op jit(solution)/shard_map/all_to_all | solution.py:68
  336.5 4.2 fusion.71
  340.7 3.6 fusion.15
  344.3 3.6 fusion.16
  348.0 2.6 fusion.22
  350.6 3.6 fusion.20
  355.0 14.4 %all-to-all-start.2 = ((f32[2,64,2]{2,0,1:T(2,128)}), f32[2,64,2]{2,0,1:T(2,128)S(1)}, u32[]{:S(2)}, u32[]{:S(2)}) async-start(f32[2,64,2]{2,0,1:T(2,128)} %copy.54), calls=%async_computation.2 | async-start | bytes 131072 | tf_op jit(solution)/shard_map/all_to_all | solution.py:74
  369.4 1.3 dynamic-slice
  372.1 5.0 %all-to-all-done.2 = f32[2,64,2]{2,0,1:T(2,128)S(1)} async-done(((f32[2,64,2]{2,0,1:T(2,128)}), f32[2,64,2]{2,0,1:T(2,128)S(1)}, u32[]{:S(2)}, u32[]{:S(2)}) %all-to-all-start.2) | async-done | bytes 1056 | tf_op jit(solution)/shard_map/all_to_all | solution.py:74
  377.3 41.4 %all-reduce = f32[2,2,64]{2,1,0:T(2,128)S(1)} all-reduce(f32[2,2,64]{2,1,0:T(2,128)S(1)} %all_to_all.50), channel_id=2, replica_groups=mesh['band'=32,'ga'=16] {'ga'}, use_global_device_ids=true, to_apply=%region_1.2.clone | all-reduce | flops 256 | bytes 2048
  (28 shorter events, 6.9 us)
Async XLA Ops:
  7.2 329.4 %all-gather.2.cloned.1.call-start = ((), (), s32[]{:S(2)}) async-start(), calls=%async_computation.3 | async-start | bytes 8650752 | tf_op jit(solution)/shard_map/all_gather | solution.py:71
  12.0 35.3 %all-to-all-start = ((bf16[2,2,128,256]{3,1,0,2:T(2,128)(2,1)}), bf16[2,2,128,256]{3,1,0,2:T(2,128)(2,1)S(1)}, u32[]{:S(2)}, u32[]{:S(2)}) async-start(bf16[2,2,128,256]{3,1,0,2:T(2,128)(2,1)} %copy.36), calls=%async_computation | async-start | bytes 524288 | tf_op jit(solution)/shard_map/all_to_all | solution.py:57
  188.5 23.0 %copy-start = (f32[8,128,128]{2,1,0:T(8,128)S(1)}, f32[8,128,128]{2,1,0:T(8,128)}, u32[]{:S(2)}) copy-start(f32[8,128,128]{2,1,0:T(8,128)} %param.6) | copy-start | bytes 1572868
  355.0 22.2 %all-to-all-start.2 = ((f32[2,64,2]{2,0,1:T(2,128)}), f32[2,64,2]{2,0,1:T(2,128)S(1)}, u32[]{:S(2)}, u32[]{:S(2)}) async-start(f32[2,64,2]{2,0,1:T(2,128)} %copy.54), calls=%async_computation.2 | async-start | bytes 131072 | tf_op jit(solution)/shard_map/all_to_all | solution.py:74
Sparse Core Ops, SparseCore 0:
  10.1 87.0 all-gather.1
where the time goes:
time: 433 us; the launch traced here: 426 us
  local copies, waits for them, and re-layouts  268 us (62%)
  blocking collectives  70.1 us (16%)
  starting transfers between devices  32.6 us (8%)
  other arithmetic  19 us (4%)
  matrix products  16.5 us (4%)
  between operations  14.9 us (3%)
  waiting for transfers between devices  5.06 us (1%)
    gather x2, local copies, waits for them, and re-layouts, per_device(): jnp.take(received, safe_index, axis=3)  157 us
    unnamed x1, blocking collectives  41.4 us
    gather x1, local copies, waits for them, and re-layouts, per_device(): mixed = jnp.take(flattened, stick_columns, axis=3).astype(jnp.bfloat16)  39.1 us
    all_to_all x1, blocking collectives, per_device(): mixed = lax.all_to_all(mixed, 'ga', split_axis=3, concat_axis=2, tiled=True)  28.8 us
    all_to_all x1, starting transfers between devices, per_device(): lax.all_to_all(columns_z, 'ga', split_axis=2, concat_axis=3, tiled=True)  18.2 us
    reshape x1, local copies, waits for them, and re-layouts, per_device(): flattened = final.reshape(2, members, layers, extent_x * extent_y)  17.7 us
    unnamed x1, other arithmetic  16.7 us
    unnamed x8, local copies, waits for them, and re-layouts  16.2 us
  transfers between devices with their start and end apart: 3, of which 1 were waited for; matrix products, arithmetic and copies ran while one was open for 66% of the time, Pallas kernels for 0%

commit v1 on v0

v1 whole, which is shorter than its diff:
```python
import functools
import math

import jax
import jax.numpy as jnp
import ml_dtypes
import numpy as np
from jax import lax
from jax.experimental import pallas as pl
from jax.experimental.pallas import tpu as pltpu
from jax.sharding import PartitionSpec as P

MESH = pl.DeviceIdType.MESH
F32 = jnp.float32
BF16 = jnp.bfloat16
L = 128


def section_table():
    counter = np.arange(L)
    angles = (counter[:, None] * counter[None, :] % L).astype(np.float32)
    angles = angles * np.float32(2.0 * math.pi / L)
    cosine, sine = np.cos(angles), np.sin(angles)
    return np.block([[cosine, sine], [-sine, cosine]])


def dot(left, right, over_left=1, over_right=0):
    numbers = (((over_left,), (over_right,)), ((), ()))
    return lax.dot_general(left, right, numbers, preferred_element_type=F32)


def lanes(parts):
    return jnp.concatenate(parts, axis=1)


def rows(parts):
    return jnp.concatenate(parts, axis=0)


def block(value, row, column):
    return value[row * L : (row + 1) * L, column * L : (column + 1) * L]


def one_hot(condition):
    return jnp.where(condition, 1.0, 0.0).astype(BF16)


def iota(shape, axis):
    return lax.broadcasted_iota(jnp.int32, shape, axis)


def all_to_all(axis, size, me, source, target, send_sem, recv_sem):
    for step in range(1, size):
        peer = lax.rem(me + step, size)
        pltpu.make_async_remote_copy(
            src_ref=source(peer),
            dst_ref=target(me),
            send_sem=send_sem,
            recv_sem=recv_sem,
            device_id={axis: peer},
            device_id_type=MESH,
        ).start()


def wait_all(ref, sem):
    pltpu.make_async_copy(ref, ref, sem).wait()


def kernel(
    nband, nga, spread, grid_scale,
    coeff, panel, pot, cols, tables, applied, inter,
    send1, recv1, send2, recv2, sendp, recvp, send3, recv3,
    flat, flat2, flatp, flat3, senda, recva, sendb, recvb,
    s1, r1, s2, r2, sp, rp, s3, r3, sa, ra, sb, rb,
):
    me_band = lax.axis_index("band")
    me_ga = lax.axis_index("ga")
    barrier = pltpu.get_barrier_semaphore()
    for step in range(1, nga):
        peer = lax.rem(me_ga + step, nga)
        pl.semaphore_signal(barrier, inc=1, device_id={"ga": peer}, device_id_type=MESH)
    for step in range(1, nband):
        peer = lax.rem(me_band + step, nband)
        pl.semaphore_signal(barrier, inc=1, device_id={"band": peer}, device_id_type=MESH)

    inverse, forward, along_z = tables[0], tables[1], tables[2]

    def z_in(band):
        own = lanes([coeff[0, band], coeff[1, band]])
        value = (dot(along_z, own, 1, 1) * spread).astype(BF16)
        for half in range(2):
            send1[band, :, half] = value[:, half * L : (half + 1) * L].reshape(nga, 16, L)

    z_in(0)
    pl.semaphore_wait(barrier, nga + nband - 2)

    def send_sticks(band):
        all_to_all(
            "ga", nga, me_ga,
            lambda peer: send1.at[band, peer], lambda me: recv1.at[band, me],
            s1.at[band], r1.at[band],
        )
        recv1[band, me_ga] = send1[band, me_ga]

    send_sticks(0)
    z_in(1)
    send_sticks(1)

    def pack(real, imag):
        return jnp.concatenate(
            [real.reshape(nband, 8, L), imag.reshape(nband, 8, L)], axis=1
        ).astype(BF16)

    for band in range(2):
        sendp[:, band] = pack(panel[0, band].astype(F32), panel[1, band].astype(F32))
    all_to_all(
        "band", nband, me_band,
        lambda peer: sendp.at[peer], lambda me: recvp.at[me], sp, rp,
    )
    recvp[me_band] = sendp[me_band]

    col_x = lax.shift_right_logical(cols[...], 7)
    col_y = jnp.bitwise_and(cols[...], L - 1)
    blocks = col_x.shape[0]
    sub = iota((L, L), 0)
    lane = iota((L, L), 1)
    hot_x = lanes([one_hot(sub == col_x[t : t + 1, :]) for t in range(blocks)])
    hot_y = lanes([one_hot(sub == col_y[t : t + 1, :]) for t in range(blocks)])
    there = dot(hot_x, hot_y, 1, 1).astype(BF16)
    before = one_hot(sub < lane)
    ones = jnp.ones((L, L), BF16)
    rank = dot(there, before)
    below = dot(one_hot(lane < sub), there).astype(BF16)
    start = dot(below, ones).astype(jnp.int32)
    slot = start + rank.astype(jnp.int32)
    from_lane = jnp.bitwise_and(slot, L - 1)
    present = there.astype(F32) > 0.5
    first = lax.shift_right_logical(start, 7)
    lane_first = lane >= jnp.bitwise_and(start, L - 1)
    expand = rows([one_hot(first == lane), one_hot(first + 1 == lane)])[:, :blocks]
    where = dot(expand, lanes([col_y, col_x]).astype(F32).astype(BF16))
    sel_y = jnp.where(lane_first, block(where, 0, 0), block(where, 1, 0)).astype(jnp.int32)
    sel_x = jnp.where(lane_first, block(where, 0, 1), block(where, 1, 1)).astype(jnp.int32)
    valid_first = jnp.logical_and(sel_x == sub, lane_first)
    valid_second = jnp.logical_and(sel_x == sub, jnp.logical_not(lane_first))
    count = dot(ones, there, 1, 1).astype(BF16)
    start_row = dot(count, before).astype(jnp.int32)
    first_row = lax.shift_right_logical(start_row, 7)[:blocks, :]
    sub_row = iota((blocks, L), 0)
    collect = lanes([one_hot(first_row == sub_row), one_hot(first_row + 1 == sub_row)])

    def take(value, index):
        return jnp.take_along_axis(value, index, axis=1, mode="promise_in_bounds")

    def real_space(band):
        flat[...] = recv1[band].reshape(blocks * 16, L).astype(F32)
        for pair in range(4):
            level = []
            for layer in (2 * pair, 2 * pair + 1):
                both = lanes(
                    [flat[pl.ds(c * 8 + layer, blocks, stride=16), :] for c in range(2)]
                ).astype(BF16)
                runs = dot(expand, both)
                planes = []
                for c in range(2):
                    run = jnp.where(lane_first, block(runs, 0, c), block(runs, 1, c))
                    planes.append(jnp.where(present, take(run, from_lane), 0.0).astype(BF16))
                level.append(dot(lanes(planes), inverse).astype(BF16))
            turned = rows([lanes([one[:, c * L : (c + 1) * L] for one in level]) for c in range(2)])
            local = lanes([pot[2 * pair], pot[2 * pair + 1]])
            product = (dot(forward, turned) * rows([local, local])).astype(BF16)
            turned = rows([lanes([block(product, e, p) for e in range(2)]) for p in range(2)])
            half = dot(turned, forward).astype(BF16)
            turned = rows([lanes([block(half, p, c) for p in range(2)]) for c in range(2)])
            final = (dot(inverse, turned) * grid_scale).astype(BF16).astype(F32)
            for p in range(2):
                picks = []
                for e in range(2):
                    got = take(block(final, e, p), sel_y)
                    picks.append(
                        rows(
                            [
                                jnp.where(valid_first, got, 0.0).astype(BF16),
                                jnp.where(valid_second, got, 0.0).astype(BF16),
                            ]
                        )
                    )
                sticks = dot(collect, lanes(picks))
                for e in range(2):
                    flat2[pl.ds(e * 8 + 2 * pair + p, blocks, stride=16), :] = sticks[
                        :, e * L : (e + 1) * L
                    ]
        send2[band] = flat2[...].reshape(nga, 2, 16, L).astype(BF16)

    for band in range(2):
        wait_all(recv1.at[band, pl.ds(0, nga - 1)], r1.at[band])
        real_space(band)
        all_to_all(
            "ga", nga, me_ga,
            lambda peer: send2.at[band, peer], lambda me: recv2.at[band, me],
            s2.at[band], r2.at[band],
        )
        recv2[band, me_ga] = send2[band, me_ga]

    wait_all(recvp.at[pl.ds(0, nband - 1)], rp)
    flatp[...] = recvp[...].reshape(nband * 32, L).astype(F32)
    left = lanes(
        [
            rows([flatp[pl.ds(b * 16 + j, nband, stride=32), :] for b in range(2)])
            for j in range(16)
        ]
    ).astype(BF16)

    for band in range(2):
        wait_all(recv2.at[band, pl.ds(0, nga - 1)], r2.at[band])
        own = lanes([recv2[band, :, half].reshape(nga * 16, L) for half in range(2)])
        result = dot(own, along_z, 0, 0)
        for e in range(2):
            applied[e, band] = result[:, e * L : (e + 1) * L].astype(BF16)
        send3[:, band] = pack(result[:, :L], result[:, L:])
        all_to_all(
            "band", nband, me_band,
            lambda peer: send3.at[peer, band], lambda me: recv3.at[me, band],
            s3.at[band], r3.at[band],
        )
        recv3[me_band, band] = send3[me_band, band]
    for band in range(2):
        wait_all(recv3.at[pl.ds(0, nband - 1), band], r3.at[band])

    flat3[...] = recv3[...].reshape(nband * 32, L).astype(F32)
    parts = [flat3[pl.ds(j, nband * 2, stride=16), :].astype(BF16) for j in range(16)]
    right = rows([lanes(parts), lanes(parts[8:] + [-one for one in parts[:8]])])
    value = dot(left, right, 1, 1) * spread
    senda[:, 0, :] = value[:nband]
    senda[:, 1, :] = value[nband:]
    all_to_all(
        "band", nband, me_band,
        lambda peer: senda.at[peer], lambda me: recva.at[me], sa, ra,
    )
    recva[me_band] = senda[me_band]
    wait_all(recva.at[pl.ds(0, nband - 1)], ra)
    sendb[...] = jnp.sum(recva[...], axis=0)
    all_to_all(
        "ga", nga, me_ga,
        lambda peer: sendb, lambda me: recvb.at[me], sb, rb,
    )
    recvb[me_ga] = sendb[...]
    wait_all(recvb.at[pl.ds(0, nga - 1)], rb)
    total = jnp.sum(recvb[...], axis=0)
    total = rows([total, jnp.zeros((6, L), F32)])
    width = inter.shape[2]
    for e in range(2):
        index = jnp.bitwise_and(iota((8, L), 1) + (e * (L // 2) + me_ga * width), L - 1)
        inter[e] = take(total, index)[:2, :width]

    for band in range(2):
        wait_all(send1.at[band, pl.ds(0, nga - 1)], s1.at[band])
        wait_all(send2.at[band, pl.ds(0, nga - 1)], s2.at[band])
        wait_all(send3.at[pl.ds(0, nband - 1), band], s3.at[band])
    wait_all(sendp.at[pl.ds(0, nband - 1)], sp)
    wait_all(senda.at[pl.ds(0, nband - 1)], sa)
    wait_all(recvb.at[pl.ds(0, nga - 1)], sb)


def solution(mesh):
    nband, nga = mesh.shape["band"], mesh.shape["ga"]

    def per_device(coefficients, panel, potential, stick_columns):
        sticks = stick_columns.shape[0]
        depth = coefficients.shape[3]
        spread = 1.0 / math.sqrt(sticks * depth)
        grid_scale = 1.0 / math.sqrt(L * L * depth)
        inverse = section_table()
        layers = L // nga
        along_z = inverse.T.reshape(2, nga, layers, 2 * L).transpose(1, 0, 2, 3)
        tables = np.stack([inverse, inverse.T, along_z.reshape(2 * L, 2 * L)])
        vmem = pl.BlockSpec(memory_space=pltpu.VMEM)
        dma = pltpu.SemaphoreType.DMA
        applied, intersection = pl.pallas_call(
            functools.partial(kernel, nband, nga, spread, grid_scale),
            out_shape=(
                jax.ShapeDtypeStruct(coefficients.shape, BF16),
                jax.ShapeDtypeStruct((2, 2, 2 * nband // nga), F32),
            ),
            in_specs=[vmem] * 5,
            out_specs=(vmem, vmem),
            scratch_shapes=[
                pltpu.VMEM((2, nga, 2, 16, L), BF16),
                pltpu.VMEM((2, nga, 2, 16, L), BF16),
                pltpu.VMEM((2, nga, 2, 16, L), BF16),
                pltpu.VMEM((2, nga, 2, 16, L), BF16),
                pltpu.VMEM((nband, 2, 16, L), BF16),
                pltpu.VMEM((nband, 2, 16, L), BF16),
                pltpu.VMEM((nband, 2, 16, L), BF16),
                pltpu.VMEM((nband, 2, 16, L), BF16),
                pltpu.VMEM((nga * 32, L), F32),
                pltpu.VMEM((nga * 32, L), F32),
                pltpu.VMEM((nband * 32, L), F32),
                pltpu.VMEM((nband * 32, L), F32),
                pltpu.VMEM((nband, 2, L), F32),
                pltpu.VMEM((nband, 2, L), F32),
                pltpu.VMEM((2, L), F32),
                pltpu.VMEM((nga, 2, L), F32),
                dma((2,)), dma((2,)), dma((2,)), dma((2,)), dma, dma,
                dma((2,)), dma((2,)), dma, dma, dma, dma,
            ],
            compiler_params=pltpu.CompilerParams(
                collective_id=0, has_side_effects=True, vmem_limit_bytes=48 * 2**20
            ),
        )(
            coefficients,
            panel,
            potential,
            stick_columns.reshape(sticks // L, L),
            jnp.asarray(tables.astype(ml_dtypes.bfloat16)),
        )
        return applied, intersection

    in_specs = (P(None, "band", "ga", None), P(None, "band", "ga", None), P("ga", None, None), P())
    out_specs = (P(None, "band", "ga", None), P(None, "band", "ga"))
    return jax.shard_map(
        per_device, mesh=mesh, in_specs=in_specs, out_specs=out_specs, check_vma=False
    )
```

time: 433 us -> 78.3 us (0.18); the launches traced: 426 us -> 78 us
  local copies, waits for them, and re-layouts: 268 us -> 5.93 us
  Pallas kernels: 0 us -> 71.4 us
  blocking collectives: 70.1 us -> 0 us
  starting transfers between devices: 32.6 us -> 0 us
  other arithmetic: 19 us -> 0 us
  matrix products: 16.5 us -> 0 us
  between operations: 14.9 us -> 0.65 us
  waiting for transfers between devices: 5.06 us -> 0 us
    gather x3 -> x0, local copies, waits for them, and re-layouts: 196 us -> none  [the longest x2 157 us: per_device(): jnp.take(received, safe_index, axis=3)]
    pallas_call x0 -> x1, Pallas kernels: none -> 71.4 us  [per_device(): pl.pallas_call(functools.partial(kernel, nband, nga, spread, grid_scale),...]
    unnamed x1 -> x0, blocking collectives: 41.4 us -> none
    all_to_all x2 -> x0, starting transfers between devices: 32.6 us -> none  [the longest x1 18.2 us: per_device(): lax.all_to_all(columns_z, 'ga', split_axis=2, concat_axis=3, tiled=True)]
    all_to_all x1 -> x0, blocking collectives: 28.8 us -> none  [per_device(): mixed = lax.all_to_all(mixed, 'ga', split_axis=3, concat_axis=2, tiled=True)]
    reshape x1 -> x0, local copies, waits for them, and re-layouts: 17.7 us -> none  [per_device(): flattened = final.reshape(2, members, layers, extent_x * extent_y)]
    unnamed x1 -> x0, other arithmetic: 16.7 us -> none
    dot_general x8 -> x0, matrix products: 16.5 us -> none  [the longest x4 13.5 us: contract(): lax.dot_general(one_side, other_side, numbers, preferred_element_type=jnp...]
  transfers between devices with their start and end apart: 3 -> 0, of which waited for: 1 -> 0; matrix products, arithmetic and copies ran while one was open for 66% -> 0% of each run, Pallas kernels for 0% -> 0%
where the time goes in v1:
time: 78.3 us; the launch traced here: 78 us
  Pallas kernels  71.4 us (91%)
  local copies, waits for them, and re-layouts  5.93 us (8%)
    pallas_call x1, Pallas kernels, per_device(): pl.pallas_call(functools.partial(kernel, nband, nga, spread, grid_scale),...  71.4 us
    unnamed x12, local copies, waits for them, and re-layouts  5.93 us

profile of v1, /device:TPU:1, one launch (start us, length us, event | category | flops | bytes accessed | tf_op | source)
XLA Modules:
  0.0 78.0 jit_solution(14687599387797203338)
XLA Ops:
  0.6 0.0 copy-start
  0.6 1.0 %copy-done = f32[8,128,128]{2,1,0:T(8,128)S(1)} copy-done((f32[8,128,128]{2,1,0:T(8,128)S(1)}, f32[8,128,128]{2,1,0:T(8,128)}, u32[]{:S(2)}) %copy-start) | copy-done | bytes 524312
  1.7 0.0 copy-start.1
  1.7 1.0 %copy-done.1 = bf16[3,256,256]{2,1,0:T(8,128)(2,1)S(1)} copy-done((bf16[3,256,256]{2,1,0:T(8,128)(2,1)S(1)}, bf16[3,256,256]{2,1,0:T(8,128)(2,1)}, u32[]{:S(2)}) %copy-start.1) | copy-done | bytes 393240
  2.7 0.0 copy-start.2
  2.7 0.9 %copy-done.2 = bf16[2,2,256,128]{3,2,1,0:T(8,128)(2,1)S(1)} copy-done((bf16[2,2,256,128]{3,2,1,0:T(8,128)(2,1)S(1)}, bf16[2,2,256,128]{3,2,1,0:T(8,128)(2,1)}, u32[]{:S(2)}) %copy-start.2) | copy-done | bytes 262168
  3.6 0.0 copy-start.3
  3.6 0.9 %copy-done.3 = bf16[2,2,256,128]{3,2,1,0:T(8,128)(2,1)S(1)} copy-done((bf16[2,2,256,128]{3,2,1,0:T(8,128)(2,1)S(1)}, bf16[2,2,256,128]{3,2,1,0:T(8,128)(2,1)}, u32[]{:S(2)}) %copy-start.3) | copy-done | bytes 262168
  4.6 0.0 copy-start.4
  4.6 0.7 copy-done.4
  5.3 71.4 %shard_map.68 = (bf16[2,2,256,128]{3,2,1,0:T(8,128)(2,1)S(1)}, f32[2,2,4]{2,1,0:T(2,128)S(1)}) custom-call(bf16[2,2,256,128]{3,2,1,0:T(8,128)(2,1)S(1)} %copy-done.2, bf16[2,2,256,128]{3,2,1,0:T(8,128)(2,1)S(1)} %copy-done.3, f32[8,128,128]{2,1,0:T(8,128)S(1)} %copy-done, s32[32,128]{1,0:T(8,128)S(1)} %bitcast.1, bf16[3,256,256]{2,1,0:T(8,128)(2,1)S(1)} %copy-done.1), custom_call_target="tpu_custom_call" | custom-call | tf_op jit(solution)/shard_map/pallas_call | solution.py:279
  76.7 0.7 copy.9
  77.4 0.6 copy.10
Async XLA Ops:
  0.6 1.0 %copy-start = (f32[8,128,128]{2,1,0:T(8,128)S(1)}, f32[8,128,128]{2,1,0:T(8,128)}, u32[]{:S(2)}) copy-start(f32[8,128,128]{2,1,0:T(8,128)} %pot.1) | copy-start | bytes 1572868
  1.7 1.0 %copy-start.1 = (bf16[3,256,256]{2,1,0:T(8,128)(2,1)S(1)}, bf16[3,256,256]{2,1,0:T(8,128)(2,1)}, u32[]{:S(2)}) copy-start(bf16[3,256,256]{2,1,0:T(8,128)(2,1)} %constant.2.clone.tables) | copy-start | bytes 1179652
  2.7 0.9 %copy-start.2 = (bf16[2,2,256,128]{3,2,1,0:T(8,128)(2,1)S(1)}, bf16[2,2,256,128]{3,2,1,0:T(8,128)(2,1)}, u32[]{:S(2)}) copy-start(bf16[2,2,256,128]{3,2,1,0:T(8,128)(2,1)} %coeff.1) | copy-start | bytes 786436
  3.6 0.9 %copy-start.3 = (bf16[2,2,256,128]{3,2,1,0:T(8,128)(2,1)S(1)}, bf16[2,2,256,128]{3,2,1,0:T(8,128)(2,1)}, u32[]{:S(2)}) copy-start(bf16[2,2,256,128]{3,2,1,0:T(8,128)(2,1)} %panel.1) | copy-start | bytes 786436
  4.6 0.7 copy-start.4

commit v2 on v1

v2 whole, which is shorter than its diff:
```python
import functools
import math

import jax
import jax.numpy as jnp
import ml_dtypes
import numpy as np
from jax import lax
from jax.experimental import pallas as pl
from jax.experimental.pallas import tpu as pltpu
from jax.sharding import PartitionSpec as P

MESH = pl.DeviceIdType.MESH
F32 = jnp.float32
BF16 = jnp.bfloat16
L = 128


def section_table():
    counter = np.arange(L)
    angles = (counter[:, None] * counter[None, :] % L).astype(np.float32)
    angles = angles * np.float32(2.0 * math.pi / L)
    cosine, sine = np.cos(angles), np.sin(angles)
    return np.block([[cosine, sine], [-sine, cosine]])


def dot(left, right, over_left=1, over_right=0):
    numbers = (((over_left,), (over_right,)), ((), ()))
    return lax.dot_general(left, right, numbers, preferred_element_type=F32)


def lanes(parts):
    return jnp.concatenate(parts, axis=1)


def rows(parts):
    return jnp.concatenate(parts, axis=0)


def block(value, row, column):
    return value[row * L : (row + 1) * L, column * L : (column + 1) * L]


def one_hot(condition):
    return jnp.where(condition, 1.0, 0.0).astype(BF16)


def iota(shape, axis):
    return lax.broadcasted_iota(jnp.int32, shape, axis)


def order(axis, size):
    if axis != "ga":
        return list(range(1, size))
    return [(z, x) for z in (2, 1, 3, 0) for x in range(4) if z or x]


def all_to_all(axis, size, me, source, target, send_sem, recv_sem):
    for step in order(axis, size):
        if isinstance(step, tuple):
            peer = lax.rem(me // 4 + step[0], 4) * 4 + lax.rem(lax.rem(me, 4) + step[1], 4)
        else:
            peer = lax.rem(me + step, size)
        pltpu.make_async_remote_copy(
            src_ref=source(peer),
            dst_ref=target(me),
            send_sem=send_sem,
            recv_sem=recv_sem,
            device_id={axis: peer},
            device_id_type=MESH,
        ).start()


def wait_all(ref, sem):
    pltpu.make_async_copy(ref, ref, sem).wait()


def kernel(
    nband, nga, spread, grid_scale,
    coeff_hbm, panel_hbm, pot_hbm, cols_hbm, tables_hbm, applied, inter,
    coeff, panel, pot, cols, cols_s, tables, first_v, first_s, window, place,
    send1, recv1, send2, recv2, sendp, recvp, recv3,
    flat, grid, picked, stage, flatp, flat3, senda, recva, sendb, recvb,
    load, s1, r1, s2, r2, sp, rp, s3, r3, sa, ra, sb, rb,
):
    loads = [
        pltpu.make_async_copy(source, target, load.at[i])
        for i, (source, target) in enumerate(
            [
                (coeff_hbm, coeff),
                (tables_hbm, tables),
                (cols_hbm, cols),
                (cols_hbm, cols_s),
                (panel_hbm, panel),
                (pot_hbm, pot),
            ]
        )
    ]
    for copy in loads:
        copy.start()
    me_band = lax.axis_index("band")
    me_ga = lax.axis_index("ga")
    barrier = pltpu.get_barrier_semaphore()
    for step in range(1, nga):
        peer = lax.rem(me_ga + step, nga)
        pl.semaphore_signal(barrier, inc=1, device_id={"ga": peer}, device_id_type=MESH)
    for step in range(1, nband):
        peer = lax.rem(me_band + step, nband)
        pl.semaphore_signal(barrier, inc=1, device_id={"band": peer}, device_id_type=MESH)

    loads[0].wait()
    loads[1].wait()
    inverse, forward = tables[0], tables[1]

    def z_section(source, band):
        value = dot(tables[2], lanes([source[0, band], source[1, band]]), 1, 1)
        return [value[:, t * L : (t + 1) * L].reshape(nga * 2, 8, L) for t in range(2)]

    def tiles(parts):
        return jnp.concatenate(parts, axis=1).astype(BF16)

    def z_in(band):
        send1[band] = tiles([one * spread for one in z_section(coeff, band)])

    z_in(0)
    pl.semaphore_wait(barrier, nga + nband - 2)

    def send_sticks(band):
        for half in range(2):
            all_to_all(
                "ga", nga, me_ga,
                lambda peer: send1.at[band, peer * 2 + half], lambda me: recv1.at[band, half, me],
                s1.at[band, half], r1.at[band, half],
            )
            recv1[band, half, me_ga] = send1[band, me_ga * 2 + half]

    send_sticks(0)
    z_in(1)
    send_sticks(1)

    loads[4].wait()
    for band in range(2):
        sendp[:, band] = tiles(z_section(panel, band))
    all_to_all(
        "band", nband, me_band,
        lambda peer: sendp.at[peer], lambda me: recvp.at[me], sp, rp,
    )
    recvp[me_band] = sendp[me_band]

    loads[2].wait()
    loads[3].wait()
    col_x = lax.shift_right_logical(cols[...], 7)
    col_y = jnp.bitwise_and(cols[...], L - 1)
    blocks = col_x.shape[0]
    sub = iota((L, L), 0)
    lane = iota((L, L), 1)
    hot_x = lanes([one_hot(sub == col_x[t : t + 1, :]) for t in range(blocks)])
    hot_y = lanes([one_hot(sub == col_y[t : t + 1, :]) for t in range(blocks)])
    there = dot(hot_x, hot_y, 1, 1).astype(BF16)
    before = one_hot(sub < lane)
    ones = jnp.ones((L, L), BF16)
    rank = dot(there, before)
    below = dot(one_hot(lane < sub), there).astype(BF16)
    start = dot(below, ones).astype(jnp.int32)
    slot = start + rank.astype(jnp.int32)
    from_lane = jnp.bitwise_and(slot, L - 1)
    present = there.astype(F32) > 0.5
    first = lax.shift_right_logical(start, 7)
    lane_first = lane >= jnp.bitwise_and(start, L - 1)
    window[...] = jnp.where(lane_first, 1, 0)
    expand = rows([one_hot(first == lane), one_hot(first + 1 == lane)])[:, :blocks]
    where = dot(expand, lanes([col_y, col_x]).astype(F32).astype(BF16))
    sel_y = jnp.where(lane_first, block(where, 0, 0), block(where, 1, 0)).astype(jnp.int32)
    sel_x = jnp.where(lane_first, block(where, 0, 1), block(where, 1, 1)).astype(jnp.int32)
    place[...] = jnp.where(sel_x == sub, jnp.where(lane_first, 1, 2), 0)
    count = dot(ones, there, 1, 1).astype(BF16)
    start_row = dot(count, before)[:8].astype(jnp.int32)
    first_v[...] = jnp.minimum(lax.shift_right_logical(start_row, 7), blocks)
    to_scalars = pltpu.make_async_copy(first_v, first_s, load.at[6])
    to_scalars.start()
    flat[blocks:] = jnp.zeros((2, 8, L), F32)
    to_scalars.wait()

    def take(value, index):
        return jnp.take_along_axis(value, index, axis=1, mode="promise_in_bounds")

    def real_space(band, half):
        flat[:blocks] = recv1[band, half].astype(F32).reshape(blocks, 8, L)
        for x in range(L):
            at = first_s[0, x]
            grid[x * 8 : (x + 1) * 8, :] = jnp.where(
                window[x : x + 1, :] == 1, flat[at], flat[at + 1]
            )
        for pair in range(2):
            level = []
            for layer in (2 * pair, 2 * pair + 1):
                planes = []
                for c in range(2):
                    run = grid[pl.ds(c * 4 + layer, L, stride=8), :]
                    planes.append(jnp.where(present, take(run, from_lane), 0.0).astype(BF16))
                level.append(dot(lanes(planes), inverse).astype(BF16))
            turned = rows([lanes([one[:, c * L : (c + 1) * L] for one in level]) for c in range(2)])
            local = lanes([pot[4 * half + 2 * pair], pot[4 * half + 2 * pair + 1]])
            product = (dot(forward, turned) * rows([local, local])).astype(BF16)
            turned = rows([lanes([block(product, e, p) for e in range(2)]) for p in range(2)])
            level = dot(turned, forward).astype(BF16)
            turned = rows([lanes([block(level, p, c) for p in range(2)]) for c in range(2)])
            final = dot(inverse, turned) * grid_scale
            for p in range(2):
                for e in range(2):
                    picked[pl.ds(e * 4 + 2 * pair + p, L, stride=8), :] = take(
                        block(final, e, p), sel_y
                    )
        held = jnp.zeros((8, L), F32)
        for x in range(L):
            row = picked[x * 8 : (x + 1) * 8, :]
            part = place[x : x + 1, :]
            held = jnp.where(part == 1, row, held)
            stage[x] = held
            held = jnp.where(part == 2, row, held)
        for peer in range(nga):
            both = [
                stage[lax.shift_right_logical(cols_s[t, L - 1], 7)] for t in (2 * peer, 2 * peer + 1)
            ]
            send2[band, half, peer] = rows(both).astype(BF16)

    loads[5].wait()
    chunks = [(band, half) for band in range(2) for half in range(2)]
    for band, half in chunks:
        wait_all(recv1.at[band, half, pl.ds(0, nga - 1)], r1.at[band, half])
        real_space(band, half)
        all_to_all(
            "ga", nga, me_ga,
            lambda peer: send2.at[band, half, peer], lambda me: recv2.at[band, half, me],
            s2.at[band, half], r2.at[band, half],
        )
        recv2[band, half, me_ga] = send2[band, half, me_ga]

    order_j = [t * 8 + e * 4 + layer for e in range(2) for t in range(2) for layer in range(4)]
    wait_all(recvp.at[pl.ds(0, nband - 1)], rp)
    flatp[...] = recvp[...].reshape(nband * 32, L).astype(F32)
    left = lanes(
        [
            rows([flatp[pl.ds(b * 16 + j, nband, stride=32), :] for b in range(2)])
            for j in order_j
        ]
    ).astype(BF16)

    def forward_copy(band, half, member):
        target = member * 2 + half
        return pltpu.make_async_remote_copy(
            src_ref=recv2.at[band, half, member],
            dst_ref=recv3.at[me_band, band],
            send_sem=s3.at[band],
            recv_sem=r3.at[band],
            device_id={"band": target},
            device_id_type=MESH,
        )

    for band, half in chunks:
        wait_all(recv2.at[band, half, pl.ds(0, nga - 1)], r2.at[band, half])
        mine = lax.rem(me_band, 2) == half
        for step in range(1, nga):
            forward_copy(band, half, lax.rem(me_band // 2 + step, nga)).start()

        @pl.when(jnp.logical_not(mine))
        def _():
            forward_copy(band, half, me_band // 2).start()

        @pl.when(mine)
        def _():
            recv3[me_band, band] = recv2[band, half, me_band // 2]

    for band in range(2):
        own = rows(
            [
                lanes([recv2[band, half].astype(F32)[:, t * 8 : t * 8 + 8].reshape(L, L) for t in range(2)])
                for half in range(2)
            ]
        ).astype(BF16)
        result = dot(own, tables[3], 0, 0).astype(BF16)
        for e in range(2):
            applied[e, band] = result[:, e * L : (e + 1) * L]
    for band in range(2):
        wait_all(recv3.at[pl.ds(0, nband - 1), band], r3.at[band])

    flat3[...] = recv3[...].reshape(nband * 32, L).astype(F32)
    parts = [flat3[pl.ds(j, nband * 2, stride=16), :].astype(BF16) for j in order_j]
    right = rows([lanes(parts), lanes(parts[8:] + [-one for one in parts[:8]])])
    value = dot(left, right, 1, 1) * spread
    senda[:, 0, :] = value[:nband]
    senda[:, 1, :] = value[nband:]
    all_to_all(
        "band", nband, me_band,
        lambda peer: senda.at[peer], lambda me: recva.at[me], sa, ra,
    )
    recva[me_band] = senda[me_band]
    wait_all(recva.at[pl.ds(0, nband - 1)], ra)
    sendb[...] = jnp.sum(recva[...], axis=0)
    all_to_all(
        "ga", nga, me_ga,
        lambda peer: sendb, lambda me: recvb.at[me], sb, rb,
    )
    recvb[me_ga] = sendb[...]
    wait_all(recvb.at[pl.ds(0, nga - 1)], rb)
    total = jnp.sum(recvb[...], axis=0)
    total = rows([total, jnp.zeros((6, L), F32)])
    width = inter.shape[2]
    for e in range(2):
        index = jnp.bitwise_and(iota((8, L), 1) + (e * (L // 2) + me_ga * width), L - 1)
        inter[e] = take(total, index)[:2, :width]

    for band in range(2):
        for half in range(2):
            wait_all(send1.at[band, pl.ds(0, nga - 1)], s1.at[band, half])
            wait_all(send2.at[band, half, pl.ds(0, nga - 1)], s2.at[band, half])
        wait_all(recv3.at[pl.ds(0, nband - 1), band], s3.at[band])
    wait_all(sendp.at[pl.ds(0, nband - 1)], sp)
    wait_all(senda.at[pl.ds(0, nband - 1)], sa)
    wait_all(recvb.at[pl.ds(0, nga - 1)], sb)


def solution(mesh):
    nband, nga = mesh.shape["band"], mesh.shape["ga"]

    def per_device(coefficients, panel, potential, stick_columns):
        sticks = stick_columns.shape[0]
        depth = coefficients.shape[3]
        spread = 1.0 / math.sqrt(sticks * depth)
        grid_scale = 1.0 / math.sqrt(L * L * depth)
        inverse = section_table()
        split = inverse.T.reshape(2, nga, 2, 4, 2 * L)
        orders = [split.transpose(1, 2, 0, 3, 4), split.transpose(2, 1, 0, 3, 4)]
        tables = np.stack([inverse, inverse.T] + [one.reshape(2 * L, 2 * L) for one in orders])
        vmem = pl.BlockSpec(memory_space=pltpu.VMEM)
        hbm = pl.BlockSpec(memory_space=pl.ANY)
        blocks = sticks // L
        dma = pltpu.SemaphoreType.DMA
        applied, intersection = pl.pallas_call(
            functools.partial(kernel, nband, nga, spread, grid_scale),
            out_shape=(
                jax.ShapeDtypeStruct(coefficients.shape, BF16),
                jax.ShapeDtypeStruct((2, 2, 2 * nband // nga), F32),
            ),
            in_specs=[hbm] * 5,
            out_specs=(vmem, vmem),
            scratch_shapes=[
                pltpu.VMEM(coefficients.shape, BF16),
                pltpu.VMEM(panel.shape, BF16),
                pltpu.VMEM(potential.shape, F32),
                pltpu.VMEM((blocks, L), jnp.int32),
                pltpu.SMEM((blocks, L), jnp.int32),
                pltpu.VMEM(tables.shape, BF16),
                pltpu.VMEM((8, L), jnp.int32),
                pltpu.SMEM((8, L), jnp.int32),
                pltpu.VMEM((L, L), jnp.int32),
                pltpu.VMEM((L, L), jnp.int32),
                pltpu.VMEM((2, nga * 2, 16, L), BF16),
                pltpu.VMEM((2, 2, nga, 16, L), BF16),
                pltpu.VMEM((2, 2, nga, 16, L), BF16),
                pltpu.VMEM((2, 2, nga, 16, L), BF16),
                pltpu.VMEM((nband, 2, 16, L), BF16),
                pltpu.VMEM((nband, 2, 16, L), BF16),
                pltpu.VMEM((nband, 2, 16, L), BF16),
                pltpu.VMEM((blocks + 2, 8, L), F32),
                pltpu.VMEM((L * 8, L), F32),
                pltpu.VMEM((L * 8, L), F32),
                pltpu.VMEM((L, 8, L), F32),
                pltpu.VMEM((nband * 32, L), F32),
                pltpu.VMEM((nband * 32, L), F32),
                pltpu.VMEM((nband, 2, L), F32),
                pltpu.VMEM((nband, 2, L), F32),
                pltpu.VMEM((2, L), F32),
                pltpu.VMEM((nga, 2, L), F32),
                dma((7,)), dma((2, 2)), dma((2, 2)), dma((2, 2)), dma((2, 2)), dma, dma,
                dma((2,)), dma((2,)), dma, dma, dma, dma,
            ],
            compiler_params=pltpu.CompilerParams(
                collective_id=0, has_side_effects=True, vmem_limit_bytes=63 * 2**20
            ),
        )(
            coefficients,
            panel,
            potential,
            stick_columns.reshape(sticks // L, L),
            jnp.asarray(tables.astype(ml_dtypes.bfloat16)),
        )
        return applied, intersection

    in_specs = (P(None, "band", "ga", None), P(None, "band", "ga", None), P("ga", None, None), P())
    out_specs = (P(None, "band", "ga", None), P(None, "band", "ga"))
    return jax.shard_map(
        per_device, mesh=mesh, in_specs=in_specs, out_specs=out_specs, check_vma=False
    )
```

time: 78.3 us -> 73.1 us (0.934)
  local copies, waits for them, and re-layouts: 5.93 us -> 2.25 us
  Pallas kernels: 71.4 us -> 70.1 us
    unnamed x12 -> x4, local copies, waits for them, and re-layouts: 5.93 us -> 2.25 us
    pallas_call x1, Pallas kernels: 71.4 us -> 70.1 us  [per_device(): pl.pallas_call(functools.partial(kernel, nband, nga, spread, grid_scale),...]
where the time goes in v2:
time: 73.1 us; the launch traced here: 73 us
  Pallas kernels  70.1 us (96%)
  local copies, waits for them, and re-layouts  2.25 us (3%)
    pallas_call x1, Pallas kernels, per_device(): pl.pallas_call(functools.partial(kernel, nband, nga, spread, grid_scale),...  70.1 us
    unnamed x4, local copies, waits for them, and re-layouts  2.25 us

profile of v2, /device:TPU:1, one launch (start us, length us, event | category | flops | bytes accessed | tf_op | source)
XLA Modules:
  0.0 73.0 jit_solution(234080008367381994)
XLA Ops:
  0.6 70.1 %shard_map.68 = (bf16[2,2,256,128]{3,2,1,0:T(8,128)(2,1)}, f32[2,2,4]{2,1,0:T(2,128)}) custom-call(bf16[2,2,256,128]{3,2,1,0:T(8,128)(2,1)} %coeff_hbm.1, bf16[2,2,256,128]{3,2,1,0:T(8,128)(2,1)} %panel_hbm.1, f32[8,128,128]{2,1,0:T(8,128)} %pot_hbm.1, s32[32,128]{1,0:T(8,128)} %bitcast.1, bf16[4,256,256]{2,1,0:T(8,128)(2,1)} %constant.2.clone.tables_hbm), custom_call_target="tpu_custom_call" | custom-call | tf_op jit(solution)/shard_map/pallas_call | solution.py:339
  70.7 0.0 copy-start
  70.7 1.7 %copy.9 = bf16[2,2,256,128]{3,2,1,0:T(8,128)(2,1)} copy(bf16[2,2,256,128]{3,2,1,0:T(8,128)(2,1)} %get-tuple-element.4) | data formatting | bytes 524288
  72.4 0.0 copy-done
  72.4 0.6 copy.10
Async XLA Ops:
  70.7 1.7 %copy-start = (f32[2,2,4]{2,1,0:T(2,128)S(1)}, f32[2,2,4]{2,1,0:T(2,128)}, u32[]{:S(2)}) copy-start(f32[2,2,4]{2,1,0:T(2,128)} %get-tuple-element.5) | copy-start | bytes 196

commit v3 on v2

v3 whole, which is shorter than its diff:
```python
import functools
import math

import jax
import jax.numpy as jnp
import ml_dtypes
import numpy as np
from jax import lax
from jax.experimental import pallas as pl
from jax.experimental.pallas import tpu as pltpu
from jax.sharding import PartitionSpec as P

MESH = pl.DeviceIdType.MESH
F32 = jnp.float32
BF16 = jnp.bfloat16
L = 128


def section_table():
    counter = np.arange(L)
    angles = (counter[:, None] * counter[None, :] % L).astype(np.float32)
    angles = angles * np.float32(2.0 * math.pi / L)
    cosine, sine = np.cos(angles), np.sin(angles)
    return np.block([[cosine, sine], [-sine, cosine]])


def dot(left, right, over_left=1, over_right=0):
    numbers = (((over_left,), (over_right,)), ((), ()))
    return lax.dot_general(left, right, numbers, preferred_element_type=F32)


def lanes(parts):
    return jnp.concatenate(parts, axis=1)


def rows(parts):
    return jnp.concatenate(parts, axis=0)


def block(value, row, column):
    return value[row * L : (row + 1) * L, column * L : (column + 1) * L]


def one_hot(condition):
    return jnp.where(condition, 1.0, 0.0).astype(BF16)


def iota(shape, axis):
    return lax.broadcasted_iota(jnp.int32, shape, axis)


def wait_all(ref, sem):
    pltpu.make_async_copy(ref, ref, sem).wait()


class Place:
    def __init__(self, nband, nga):
        self.band, self.ga = lax.axis_index("band"), lax.axis_index("ga")
        self.low = self.band // 2 % 4
        self.line = self.low * nga + self.ga
        self.side = self.band // 8 * 2 + self.band % 2
        along = [8, 7, 9, 6, 10, 5, 11, 4, 12, 3, 13, 2, 14, 1, 15, 0]
        self.steps = [(z, x) for z in along for x in range(4) if z or x]

    def line_peer(self, step):
        z = lax.rem(self.ga // 4 * 4 + self.low + step[0], 16)
        return lax.rem(z, 4), z // 4 * 4 + lax.rem(lax.rem(self.ga, 4) + step[1], 4)

    def line_id(self, low, ga):
        return {"band": self.band // 8 * 8 + low * 2 + lax.rem(self.band, 2), "ga": ga}

    def side_peer(self, step):
        return lax.rem(self.side + step, 8)

    def side_id(self, side):
        return {"band": side // 2 * 8 + self.low * 2 + lax.rem(side, 2), "ga": self.ga}


def send(source, target, send_sem, recv_sem, device):
    pltpu.make_async_remote_copy(
        src_ref=source,
        dst_ref=target,
        send_sem=send_sem,
        recv_sem=recv_sem,
        device_id=device,
        device_id_type=MESH,
    ).start()


def kernel(
    nband, nga, spread, grid_scale,
    coeff_hbm, panel_hbm, pot_hbm, cols_hbm, tables_hbm, along_hbm, applied, inter,
    coeff, panel, pot, cols, cols_s, tables, along_z, first_v, first_s, window, place,
    send1, recv1, send2, recv2, sendp, linep, recvp, recv3,
    flat, grid, picked, stage, flatp, flat3, senda, recva, sendb, recvb,
    load, s1, r1, s2, r2, sp, rp, sq, rq, s3, r3, sa, ra, sb, rb,
):
    loads = [
        pltpu.make_async_copy(source, target, load.at[i])
        for i, (source, target) in enumerate(
            [
                (coeff_hbm, coeff),
                (along_hbm, along_z),
                (cols_hbm, cols),
                (cols_hbm, cols_s),
                (panel_hbm, panel),
                (pot_hbm, pot),
                (tables_hbm, tables),
            ]
        )
    ]
    for copy in loads:
        copy.start()
    me = Place(nband, nga)
    count_line, count_side = 4 * nga, nband // 4
    barrier = pltpu.get_barrier_semaphore()
    for step in me.steps:
        device = me.line_id(*me.line_peer(step))
        pl.semaphore_signal(barrier, inc=1, device_id=device, device_id_type=MESH)
    for step in range(1, count_side):
        device = me.side_id(me.side_peer(step))
        pl.semaphore_signal(barrier, inc=1, device_id=device, device_id_type=MESH)

    def z_section(source, scale):
        own = lanes([source[part, band] for band in range(2) for part in range(2)])
        value = dot(along_z[...], own, 1, 1)
        if scale is not None:
            value = value * scale
        halves = [value[:, t * L : (t + 1) * L].reshape(count_line, 8, L) for t in range(2)]
        return jnp.concatenate(halves, axis=1).astype(BF16)

    loads[0].wait()
    loads[1].wait()
    send1[...] = z_section(coeff, spread)
    pl.semaphore_wait(barrier, count_line + count_side - 2)

    def to_slabs(source, target, send_sem, recv_sem):
        for step in me.steps:
            low, ga = me.line_peer(step)
            send(
                source.at[low * nga + ga], target.at[me.low, me.ga],
                send_sem, recv_sem.at[me.low], me.line_id(low, ga),
            )
        pltpu.make_async_copy(
            source.at[me.line], target.at[me.low, me.ga], recv_sem.at[me.low]
        ).start()

    to_slabs(send1, recv1, s1, r1)
    loads[4].wait()
    sendp[...] = z_section(panel, None)
    to_slabs(sendp, linep, sp, rp)

    loads[2].wait()
    loads[3].wait()
    col_x = lax.shift_right_logical(cols[...], 7)
    col_y = jnp.bitwise_and(cols[...], L - 1)
    blocks = col_x.shape[0]
    sub = iota((L, L), 0)
    lane = iota((L, L), 1)
    hot_x = lanes([one_hot(sub == col_x[t : t + 1, :]) for t in range(blocks)])
    hot_y = lanes([one_hot(sub == col_y[t : t + 1, :]) for t in range(blocks)])
    there = dot(hot_x, hot_y, 1, 1).astype(BF16)
    before = one_hot(sub < lane)
    ones = jnp.ones((L, L), BF16)
    rank = dot(there, before)
    below = dot(one_hot(lane < sub), there).astype(BF16)
    start = dot(below, ones).astype(jnp.int32)
    slot = start + rank.astype(jnp.int32)
    from_lane = jnp.bitwise_and(slot, L - 1)
    present = there.astype(F32) > 0.5
    first = lax.shift_right_logical(start, 7)
    lane_first = lane >= jnp.bitwise_and(start, L - 1)
    window[...] = jnp.where(lane_first, 1, 0)
    expand = rows([one_hot(first == lane), one_hot(first + 1 == lane)])[:, :blocks]
    where = dot(expand, lanes([col_y, col_x]).astype(F32).astype(BF16))
    sel_y = jnp.where(lane_first, block(where, 0, 0), block(where, 1, 0)).astype(jnp.int32)
    sel_x = jnp.where(lane_first, block(where, 0, 1), block(where, 1, 1)).astype(jnp.int32)
    place[...] = jnp.where(sel_x == sub, jnp.where(lane_first, 1, 2), 0)
    count = dot(ones, there, 1, 1).astype(BF16)
    start_row = dot(count, before)[:8].astype(jnp.int32)
    first_v[...] = jnp.minimum(lax.shift_right_logical(start_row, 7), blocks)
    to_scalars = pltpu.make_async_copy(first_v, first_s, load.at[7])
    to_scalars.start()
    flat[blocks:] = jnp.zeros((2, 8, L), F32)
    to_scalars.wait()

    def take(value, index):
        return jnp.take_along_axis(value, index, axis=1, mode="promise_in_bounds")

    def real_space(chunk):
        flat[:blocks] = recv1[chunk].astype(F32).reshape(blocks, 8, L)
        for x in range(L):
            at = first_s[0, x]
            grid[x * 8 : (x + 1) * 8, :] = jnp.where(
                window[x : x + 1, :] == 1, flat[at], flat[at + 1]
            )
        for pair in range(2):
            level = []
            for layer in range(2):
                planes = []
                for c in range(2):
                    run = grid[pl.ds(pair * 4 + c * 2 + layer, L, stride=8), :]
                    planes.append(jnp.where(present, take(run, from_lane), 0.0).astype(BF16))
                level.append(dot(lanes(planes), inverse).astype(BF16))
            turned = rows([lanes([one[:, c * L : (c + 1) * L] for one in level]) for c in range(2)])
            product = (dot(forward, turned) * rows([local, local])).astype(BF16)
            turned = rows([lanes([block(product, e, p) for e in range(2)]) for p in range(2)])
            level = dot(turned, forward).astype(BF16)
            turned = rows([lanes([block(level, p, c) for p in range(2)]) for c in range(2)])
            final = dot(inverse, turned) * grid_scale
            for p in range(2):
                for e in range(2):
                    picked[pl.ds(pair * 4 + e * 2 + p, L, stride=8), :] = take(
                        block(final, e, p), sel_y
                    )
        held = jnp.zeros((8, L), F32)
        for x in range(L):
            row = picked[x * 8 : (x + 1) * 8, :]
            part = place[x : x + 1, :]
            held = jnp.where(part == 1, row, held)
            stage[x] = held
            held = jnp.where(part == 2, row, held)
        for peer in range(nga):
            both = [
                stage[lax.shift_right_logical(cols_s[t, L - 1], 7)] for t in (2 * peer, 2 * peer + 1)
            ]
            send2[chunk, peer] = rows(both).astype(BF16)

    loads[5].wait()
    loads[6].wait()
    inverse, forward = tables[0], tables[1]
    local = lanes([pot[me.low * 2], pot[me.low * 2 + 1]])
    order_low = [2, 1, 3, 0]

    def send_picked(chunk):
        for step in range(1, count_side):
            side = me.side_peer(step)
            send(
                send2.at[chunk, pl.ds(side * 2, 2)], recv3.at[me.side, chunk],
                s3, r3, me.side_id(side),
            )
        pltpu.make_async_copy(
            send2.at[chunk, pl.ds(me.side * 2, 2)], recv3.at[me.side, chunk], r3
        ).start()

    def send_back(step_low):
        chunk = lax.rem(me.low + step_low, 4)
        for step in (2, 1, 3, 0):
            for x in range(4):
                ga = lax.rem(me.ga // 4 + step, 4) * 4 + lax.rem(lax.rem(me.ga, 4) + x, 4)
                if step_low or step or x:
                    send(send2.at[chunk, ga], recv2.at[me.line], s2, r2, me.line_id(chunk, ga))
                else:
                    pltpu.make_async_copy(send2.at[chunk, ga], recv2.at[me.line], r2).start()

    for step_low in order_low:
        chunk = lax.rem(me.low + step_low, 4)
        wait_all(recv1.at[chunk], r1.at[chunk])
        real_space(chunk)
        send_picked(chunk)

    for low in range(4):
        wait_all(linep.at[low], rp.at[low])
    for step in range(1, count_side):
        side = me.side_peer(step)
        send(linep.at[:, pl.ds(side * 2, 2)], recvp.at[me.side], sq, rq, me.side_id(side))
    pltpu.make_async_copy(linep.at[:, pl.ds(me.side * 2, 2)], recvp.at[me.side], rq).start()
    for step_low in order_low:
        send_back(step_low)

    def gram_rows(wide, part):
        taken = []
        for share in range(2):
            for t in range(2):
                for layer in range(2):
                    at = [share * 16 + t * 8 + b * 4 + part * 2 + layer for b in range(2)]
                    taken.append(rows([wide[pl.ds(one, nband, stride=32), :] for one in at]))
        return lanes(taken).astype(BF16)

    wait_all(recv3, r3)
    flat3[...] = recv3[...].astype(F32).reshape(nband * 32, L)
    right = [gram_rows(flat3, part) for part in range(2)]
    right = rows([lanes(right), lanes([right[1], -right[0]])])
    wait_all(recvp, rq)
    flatp[...] = recvp[...].astype(F32).reshape(nband * 32, L)
    left = lanes([gram_rows(flatp, part) for part in range(2)])
    value = dot(left, right, 1, 1) * spread
    for side in range(8):
        for b in range(2):
            senda[side, b * 4 : b * 4 + 4] = value[b * nband + side * 4 : b * nband + side * 4 + 4]
    for step in range(1, count_side):
        side = me.side_peer(step)
        send(senda.at[side], recva.at[me.side], sa, ra, me.side_id(side))
    recva[me.side] = senda[me.side]
    wait_all(recva.at[pl.ds(0, count_side - 1)], ra)
    summed = jnp.sum(recva[...], axis=0)
    for low in range(4):
        for b in range(2):
            sendb[low, b : b + 1] = summed[b * 4 + low : b * 4 + low + 1]
    for step in me.steps:
        low, ga = me.line_peer(step)
        send(sendb.at[low], recvb.at[me.line], sb, rb, me.line_id(low, ga))
    recvb[me.line] = sendb[me.low]

    wait_all(recv2, r2)
    got = recv2[...].astype(F32)
    own = lanes([got[:, t * 8 : t * 8 + 8].reshape(8 * count_line, L) for t in range(2)])
    result = dot(own.astype(BF16), along_z[...], 0, 0).astype(BF16)
    for band in range(2):
        for e in range(2):
            at = (band * 2 + e) * L
            applied[e, band] = result[:, at : at + L]

    wait_all(recvb.at[pl.ds(0, count_line - 1)], rb)
    total = rows([jnp.sum(recvb[...], axis=0), jnp.zeros((6, L), F32)])
    column = iota((8, L), 1)
    width = inter.shape[2]
    base = me.ga // 4 * 8 + lax.rem(me.ga, 4)
    for e in range(2):
        index = e * (L // 2) + base + lax.rem(column, 2) * 32 + lax.rem(column // 2, 2) * 4
        inter[e] = take(total, index)[:2, :width]

    wait_all(send1.at[pl.ds(0, count_line - 1)], s1)
    wait_all(send1.at[pl.ds(0, count_line - 1)], sp)
    wait_all(send1.at[pl.ds(0, count_line - 1)], s2)
    wait_all(recv3.at[pl.ds(0, count_side - 1)], s3)
    wait_all(recvp.at[pl.ds(0, count_side - 1)], sq)
    wait_all(senda.at[pl.ds(0, count_side - 1)], sa)
    wait_all(recvb.at[pl.ds(0, count_line - 1)], sb)


def solution(mesh):
    nband, nga = mesh.shape["band"], mesh.shape["ga"]

    def per_device(coefficients, panel, potential, stick_columns):
        sticks = stick_columns.shape[0]
        depth = coefficients.shape[3]
        blocks = sticks // L
        line, side = 4 * nga, nband // 4
        spread = 1.0 / math.sqrt(sticks * depth)
        grid_scale = 1.0 / math.sqrt(L * L * depth)
        inverse = section_table()
        tables = np.stack([inverse, inverse.T])
        split = inverse.T.reshape(2, nga, 4, 2, 2 * L).transpose(2, 1, 0, 3, 4)
        along = np.zeros((4, nga, 2, 2, 2, 2, 2 * L))
        for band in range(2):
            along[:, :, band, :, :, band] = split
        along = along.reshape(8 * line, 4 * L)
        vmem = pl.BlockSpec(memory_space=pltpu.VMEM)
        hbm = pl.BlockSpec(memory_space=pl.ANY)
        dma = pltpu.SemaphoreType.DMA
        line_tiles = pltpu.VMEM((line, 16, L), BF16)
        slab_tiles = pltpu.VMEM((4, nga, 16, L), BF16)
        side_tiles = pltpu.VMEM((side, 4, 2, 16, L), BF16)
        applied, intersection = pl.pallas_call(
            functools.partial(kernel, nband, nga, spread, grid_scale),
            out_shape=(
                jax.ShapeDtypeStruct(coefficients.shape, BF16),
                jax.ShapeDtypeStruct((2, 2, 2 * nband // nga), F32),
            ),
            in_specs=[hbm] * 6,
            out_specs=(vmem, vmem),
            scratch_shapes=[
                pltpu.VMEM(coefficients.shape, BF16),
                pltpu.VMEM(panel.shape, BF16),
                pltpu.VMEM(potential.shape, F32),
                pltpu.VMEM((blocks, L), jnp.int32),
                pltpu.SMEM((blocks, L), jnp.int32),
                pltpu.VMEM(tables.shape, BF16),
                pltpu.VMEM(along.shape, BF16),
                pltpu.VMEM((8, L), jnp.int32),
                pltpu.SMEM((8, L), jnp.int32),
                pltpu.VMEM((L, L), jnp.int32),
                pltpu.VMEM((L, L), jnp.int32),
                line_tiles, slab_tiles, slab_tiles, line_tiles,
                line_tiles, slab_tiles, side_tiles, side_tiles,
                pltpu.VMEM((blocks + 2, 8, L), F32),
                pltpu.VMEM((L * 8, L), F32),
                pltpu.VMEM((L * 8, L), F32),
                pltpu.VMEM((L, 8, L), F32),
                pltpu.VMEM((nband * 32, L), F32),
                pltpu.VMEM((nband * 32, L), F32),
                pltpu.VMEM((side, 8, L), F32),
                pltpu.VMEM((side, 8, L), F32),
                pltpu.VMEM((4, 2, L), F32),
                pltpu.VMEM((line, 2, L), F32),
                dma((8,)), dma, dma((4,)), dma, dma, dma, dma((4,)), dma, dma,
                dma, dma, dma, dma, dma, dma,
            ],
            compiler_params=pltpu.CompilerParams(
                collective_id=0, has_side_effects=True, vmem_limit_bytes=int(53.55 * 2**20)
            ),
        )(
            coefficients,
            panel,
            potential,
            stick_columns.reshape(blocks, L),
            jnp.asarray(tables.astype(ml_dtypes.bfloat16)),
            jnp.asarray(along.astype(ml_dtypes.bfloat16)),
        )
        return applied, intersection

    in_specs = (P(None, "band", "ga", None), P(None, "band", "ga", None), P("ga", None, None), P())
    out_specs = (P(None, "band", "ga", None), P(None, "band", "ga"))
    return jax.shard_map(
        per_device, mesh=mesh, in_specs=in_specs, out_specs=out_specs, check_vma=False
    )
```

time: 73.1 us -> 63.4 us (0.87)
  Pallas kernels: 70.1 us -> 60.5 us
    pallas_call x1, Pallas kernels: 70.1 us -> 60.5 us  [per_device(): pl.pallas_call(functools.partial(kernel, nband, nga, spread, grid_scale),...]
where the time goes in v3:
time: 63.4 us; the launch traced here: 63.1 us
  Pallas kernels  60.5 us (95%)
  local copies, waits for them, and re-layouts  1.99 us (3%)
  between operations  0.65 us (1%)
    pallas_call x1, Pallas kernels, per_device(): pl.pallas_call(functools.partial(kernel, nband, nga, spread, grid_scale),...  60.5 us
    unnamed x4, local copies, waits for them, and re-layouts  1.99 us

profile of v3, /device:TPU:1, one launch (start us, length us, event | category | flops | bytes accessed | tf_op | source)
XLA Modules:
  0.0 63.1 jit_solution(6177039578310281148)
XLA Ops:
  0.6 0.0 copy-start
  0.6 0.7 %copy-done = s32[4096]{0:T(1024)S(1)} copy-done((s32[4096]{0:T(1024)S(1)}, s32[4096]{0:T(1024)}, u32[]{:S(2)}) %copy-start) | copy-done | bytes 16408
  1.3 60.5 %shard_map.77 = (bf16[2,2,256,128]{3,2,1,0:T(8,128)(2,1)S(1)}, f32[2,2,4]{2,1,0:T(2,128)S(1)}) custom-call(bf16[2,2,256,128]{3,2,1,0:T(8,128)(2,1)} %coeff_hbm.1, bf16[2,2,256,128]{3,2,1,0:T(8,128)(2,1)} %panel_hbm.1, f32[8,128,128]{2,1,0:T(8,128)} %pot_hbm.1, s32[32,128]{1,0:T(8,128)S(1)} %bitcast.1, bf16[2,256,256]{2,1,0:T(8,128)(2,1)} %constant.4.clone.tables_hbm, ...), custom_call_target="tpu_custom_call" | custom-call | tf_op jit(solution)/shard_map/pallas_call | solution.py:355
  61.9 0.7 %copy.10 = bf16[2,2,256,128]{3,2,1,0:T(8,128)(2,1)} copy(bf16[2,2,256,128]{3,2,1,0:T(8,128)(2,1)S(1)} %get-tuple-element.4) | data formatting | bytes 524288
  62.6 0.6 copy.11
Async XLA Ops:
  0.6 0.7 %copy-start = (s32[4096]{0:T(1024)S(1)}, s32[4096]{0:T(1024)}, u32[]{:S(2)}) copy-start(s32[4096]{0:T(1024)} %param.9) | copy-start | bytes 49156

commit v4 on v3

--- a/solution.py
+++ b/solution.py
@@ -388,15 +388,20 @@
                 dma, dma, dma, dma, dma, dma,
             ],
             compiler_params=pltpu.CompilerParams(
-                collective_id=0, has_side_effects=True, vmem_limit_bytes=int(53.55 * 2**20)
+                collective_id=0, has_side_effects=True, vmem_limit_bytes=48 * 2**20
             ),
         )(
-            coefficients,
-            panel,
-            potential,
-            stick_columns.reshape(blocks, L),
-            jnp.asarray(tables.astype(ml_dtypes.bfloat16)),
-            jnp.asarray(along.astype(ml_dtypes.bfloat16)),
+            *[
+                pltpu.with_memory_space_constraint(one, pltpu.HBM)
+                for one in (
+                    coefficients,
+                    panel,
+                    potential,
+                    stick_columns.reshape(blocks, L),
+                    jnp.asarray(tables.astype(ml_dtypes.bfloat16)),
+                    jnp.asarray(along.astype(ml_dtypes.bfloat16)),
+                )
+            ]
         )
         return applied, intersection
 

time: 63.4 us -> 62.6 us (0.987)
  local copies, waits for them, and re-layouts: 1.99 us -> 1.28 us
    unnamed x4 -> x2, local copies, waits for them, and re-layouts: 1.99 us -> 1.28 us
where the time goes in v4:
time: 62.6 us; the launch traced here: 62.4 us
  Pallas kernels  60.5 us (97%)
  local copies, waits for them, and re-layouts  1.28 us (2%)
  between operations  0.64 us (1%)
    pallas_call x1, Pallas kernels, per_device(): pl.pallas_call(functools.partial(kernel, nband, nga, spread, grid_scale),...  60.5 us
    unnamed x2, local copies, waits for them, and re-layouts  1.28 us

profile of v4, /device:TPU:1, one launch (start us, length us, event | category | flops | bytes accessed | tf_op | source)
XLA Modules:
  0.0 62.4 jit_solution(782789974276029076)
XLA Ops:
  0.6 60.5 %shard_map.77 = (bf16[2,2,256,128]{3,2,1,0:T(8,128)(2,1)S(1)}, f32[2,2,4]{2,1,0:T(2,128)S(1)}) custom-call(bf16[2,2,256,128]{3,2,1,0:T(8,128)(2,1)} %coeff_hbm.1, bf16[2,2,256,128]{3,2,1,0:T(8,128)(2,1)} %panel_hbm.1, f32[8,128,128]{2,1,0:T(8,128)} %pot_hbm.1, s32[32,128]{1,0:T(8,128)} %bitcast.1, bf16[2,256,256]{2,1,0:T(8,128)(2,1)} %constant.4.clone.tables_hbm, ...), custom_call_target="tpu_custom_call" | custom-call | tf_op jit(solution)/shard_map/pallas_call | solution.py:355
  61.1 0.7 %copy.10 = bf16[2,2,256,128]{3,2,1,0:T(8,128)(2,1)} copy(bf16[2,2,256,128]{3,2,1,0:T(8,128)(2,1)S(1)} %get-tuple-element.4) | data formatting | bytes 524288
  61.8 0.6 copy.11

commit v5 on v4

--- a/solution.py
+++ b/solution.py
@@ -60,6 +60,7 @@
         self.line = self.low * nga + self.ga
         self.side = self.band // 8 * 2 + self.band % 2
         along = [8, 7, 9, 6, 10, 5, 11, 4, 12, 3, 13, 2, 14, 1, 15, 0]
+        self.side_steps = [4, 5, 3, 2, 6, 7, 1]
         self.steps = [(z, x) for z in along for x in range(4) if z or x]
 
     def line_peer(self, step):
@@ -117,7 +118,7 @@
     for step in me.steps:
         device = me.line_id(*me.line_peer(step))
         pl.semaphore_signal(barrier, inc=1, device_id=device, device_id_type=MESH)
-    for step in range(1, count_side):
+    for step in me.side_steps:
         device = me.side_id(me.side_peer(step))
         pl.semaphore_signal(barrier, inc=1, device_id=device, device_id_type=MESH)
 
@@ -132,6 +133,8 @@
     loads[0].wait()
     loads[1].wait()
     send1[...] = z_section(coeff, spread)
+    loads[4].wait()
+    sendp[...] = z_section(panel, None)
     pl.semaphore_wait(barrier, count_line + count_side - 2)
 
     def to_slabs(source, target, send_sem, recv_sem):
@@ -146,8 +149,6 @@
         ).start()
 
     to_slabs(send1, recv1, s1, r1)
-    loads[4].wait()
-    sendp[...] = z_section(panel, None)
     to_slabs(sendp, linep, sp, rp)
 
     loads[2].wait()
@@ -233,7 +234,7 @@
     order_low = [2, 1, 3, 0]
 
     def send_picked(chunk):
-        for step in range(1, count_side):
+        for step in me.side_steps:
             side = me.side_peer(step)
             send(
                 send2.at[chunk, pl.ds(side * 2, 2)], recv3.at[me.side, chunk],
@@ -261,7 +262,7 @@
 
     for low in range(4):
         wait_all(linep.at[low], rp.at[low])
-    for step in range(1, count_side):
+    for step in me.side_steps:
         side = me.side_peer(step)
         send(linep.at[:, pl.ds(side * 2, 2)], recvp.at[me.side], sq, rq, me.side_id(side))
     pltpu.make_async_copy(linep.at[:, pl.ds(me.side * 2, 2)], recvp.at[me.side], rq).start()
@@ -288,19 +289,24 @@
     for side in range(8):
         for b in range(2):
             senda[side, b * 4 : b * 4 + 4] = value[b * nband + side * 4 : b * nband + side * 4 + 4]
-    for step in range(1, count_side):
+    for step in me.side_steps:
         side = me.side_peer(step)
         send(senda.at[side], recva.at[me.side], sa, ra, me.side_id(side))
     recva[me.side] = senda[me.side]
     wait_all(recva.at[pl.ds(0, count_side - 1)], ra)
     summed = jnp.sum(recva[...], axis=0)
-    for low in range(4):
-        for b in range(2):
-            sendb[low, b : b + 1] = summed[b * 4 + low : b * 4 + low + 1]
+    column = iota((8, L), 1)
+    inner = lax.rem(column, L // 2)
+    for half in range(2):
+        index = inner // 2 * 4 + lax.rem(inner, 2) + half * 2
+        both = take(summed, index)
+        for low in range(4):
+            pair = [both[b * 4 + low : b * 4 + low + 1] for b in range(2)]
+            sendb[low, half] = jnp.where(column[:1] < L // 2, pair[0], pair[1])
     for step in me.steps:
         low, ga = me.line_peer(step)
-        send(sendb.at[low], recvb.at[me.line], sb, rb, me.line_id(low, ga))
-    recvb[me.line] = sendb[me.low]
+        send(sendb.at[low, lax.rem(ga, 4) // 2], recvb.at[me.line], sb, rb, me.line_id(low, ga))
+    recvb[me.line] = sendb[me.low, lax.rem(me.ga, 4) // 2]
 
     wait_all(recv2, r2)
     got = recv2[...].astype(F32)
@@ -312,13 +318,14 @@
             applied[e, band] = result[:, at : at + L]
 
     wait_all(recvb.at[pl.ds(0, count_line - 1)], rb)
-    total = rows([jnp.sum(recvb[...], axis=0), jnp.zeros((6, L), F32)])
-    column = iota((8, L), 1)
+    total = jnp.sum(recvb[...], axis=0)
+    total = rows([total, jnp.zeros((7, L), F32)])
     width = inter.shape[2]
-    base = me.ga // 4 * 8 + lax.rem(me.ga, 4)
+    base = me.ga // 4 * 4 + lax.rem(me.ga, 2)
     for e in range(2):
-        index = e * (L // 2) + base + lax.rem(column, 2) * 32 + lax.rem(column // 2, 2) * 4
-        inter[e] = take(total, index)[:2, :width]
+        for b in range(2):
+            index = b * 64 + e * 32 + base + lax.rem(column, 2) * 16 + lax.rem(column // 2, 2) * 2
+            inter[e, b : b + 1] = take(total, index)[:1, :width]
 
     wait_all(send1.at[pl.ds(0, count_line - 1)], s1)
     wait_all(send1.at[pl.ds(0, count_line - 1)], sp)
@@ -382,8 +389,8 @@
                 pltpu.VMEM((nband * 32, L), F32),
                 pltpu.VMEM((side, 8, L), F32),
                 pltpu.VMEM((side, 8, L), F32),
-                pltpu.VMEM((4, 2, L), F32),
-                pltpu.VMEM((line, 2, L), F32),
+                pltpu.VMEM((4, 2, 1, L), F32),
+                pltpu.VMEM((line, 1, L), F32),
                 dma((8,)), dma, dma((4,)), dma, dma, dma, dma((4,)), dma, dma,
                 dma, dma, dma, dma, dma, dma,
             ],

time: 62.6 us -> 62.4 us (level)
  no operation moved by 1% of the time
where the time goes in v5:
time: 62.4 us; the launch traced here: 62.2 us
  Pallas kernels  60.3 us (97%)
  local copies, waits for them, and re-layouts  1.28 us (2%)
  between operations  0.64 us (1%)
    pallas_call x1, Pallas kernels, per_device(): pl.pallas_call(functools.partial(kernel, nband, nga, spread, grid_scale),...  60.3 us
    unnamed x2, local copies, waits for them, and re-layouts  1.28 us

profile of v5, /device:TPU:1, one launch (start us, length us, event | category | flops | bytes accessed | tf_op | source)
XLA Modules:
  0.0 62.2 jit_solution(18187191393412199717)
XLA Ops:
  0.6 60.3 %shard_map.77 = (bf16[2,2,256,128]{3,2,1,0:T(8,128)(2,1)S(1)}, f32[2,2,4]{2,1,0:T(2,128)S(1)}) custom-call(bf16[2,2,256,128]{3,2,1,0:T(8,128)(2,1)} %coeff_hbm.1, bf16[2,2,256,128]{3,2,1,0:T(8,128)(2,1)} %panel_hbm.1, f32[8,128,128]{2,1,0:T(8,128)} %pot_hbm.1, s32[32,128]{1,0:T(8,128)} %bitcast.1, bf16[2,256,256]{2,1,0:T(8,128)(2,1)} %constant.4.clone.tables_hbm, ...), custom_call_target="tpu_custom_call" | custom-call | tf_op jit(solution)/shard_map/pallas_call | solution.py:362
  60.9 0.7 %copy.10 = bf16[2,2,256,128]{3,2,1,0:T(8,128)(2,1)} copy(bf16[2,2,256,128]{3,2,1,0:T(8,128)(2,1)S(1)} %get-tuple-element.4) | data formatting | bytes 524288
  61.6 0.6 copy.11
